TPU v7x, 512 devices: a whole 4x4x16 slice. The times are simulated.
512 devices in a mesh: tile: 32 (over z, core), mem: 16 (over y, x).
Axes of the slice: x: 4, y: 4, z: 16, core: 2. Of those that a mesh axis runs over, the one named last changes fastest.
Arguments:
- prior_ensemble: bfloat16 [256, 1048576], P('mem', 'tile'), may hold values from -6 to 6
- measurement_anomaly_matrix: bfloat16 [257, 2097152], P(None, ('tile', 'mem')), may hold values from -15 to 15, as said below
- measured_per_portion: int32 [512], replicated, may hold values from 1 to 4096, as said below
- locality_support_marks: int32 [3, 16384], replicated, may hold values 0 or 1
Outputs:
- analysis: bfloat16 [256, 1048576], P(None, ('tile', 'mem'))
Inputs may be any that keep to these rules, and one draw needn't show every extreme that they name: `measurement_anomaly_matrix`: scaled perturbations and innovations of real value; slots past a shard's count are padding. `measured_per_portion`: shard g holds slots g * 4096 to (g + 1) * 4096 - 1 of the whole, its live ones first; some shard is full in every draw.
All inputs are finite; a program needn't handle non-finite values. Where the computation divides by a largest or mean magnitude, that divisor is 1e-20 or more.
Results may differ from a plain program's by a relative error of at most 0.0061.
Values may be sent and summed in bfloat16 or wider, within the bound.
A program may use at most 64 MiB of HBM per device.

v0:
```python
import jax
import jax.numpy as jnp
from jax import lax
from jax.sharding import PartitionSpec as P

NS_STEPS = 8


loc_width = 1.0


def with_halo(cells, sides, width):
    for axis, dim in sides:
        count = lax.axis_size(axis)
        head = lax.slice_in_dim(cells, 0, width, axis=dim)
        tail = lax.slice_in_dim(cells, cells.shape[dim] - width, cells.shape[dim], axis=dim)
        cells = jnp.concatenate(
            [
                lax.ppermute(tail, axis, [(i, (i + 1) % count) for i in range(count)]),
                cells,
                lax.ppermute(head, axis, [((i + 1) % count, i) for i in range(count)]),
            ],
            axis=dim,
        )
    return cells


def shard_weights(
    locality_support_marks, measured_per_portion, source_tile, mem_index, offset, obs_dev, mem_count
):
    obs_tile = obs_dev * mem_count
    slot_index = jnp.arange(obs_dev, dtype=jnp.int32)
    alive_mask = slot_index < measured_per_portion[source_tile * mem_count + mem_index]
    first_block = (source_tile * obs_tile + mem_index * obs_dev) // 128
    block_marks = lax.dynamic_slice_in_dim(
        locality_support_marks[offset], first_block, obs_dev // 128, 0
    )
    pattern_rows = jnp.repeat(block_marks, 128)
    position = ((mem_index * obs_dev + slot_index).astype(jnp.float32) + 0.5) / obs_tile
    distance = offset - 1 + position - 0.5
    smooth = jnp.exp(-0.5 * (distance / loc_width) * (distance / loc_width))
    return jnp.where(alive_mask & (pattern_rows > 0), smooth, jnp.zeros_like(smooth))


def gram_part(columns, root_weight):
    scaled = (columns * root_weight[None, :]).astype(jnp.bfloat16)
    return lax.dot_general(
        scaled, scaled, (((1,), (1,)), ((), ())), preferred_element_type=jnp.float32
    )


def mixing_matrix(products, members):
    gram_block = products[:members, :members]
    drive_vector = products[:members, members]
    identity = jnp.eye(members, dtype=jnp.float32)
    system = (members - 1.0) * identity + gram_block
    bound_scale = jnp.max(jnp.sum(jnp.abs(system), axis=1))
    iterate = system / bound_scale
    inverse_root = identity
    for sweep_index in range(NS_STEPS):
        factor = 1.5 * identity - 0.5 * jnp.dot(
            inverse_root, iterate, precision=lax.Precision.HIGHEST
        )
        iterate = jnp.dot(iterate, factor, precision=lax.Precision.HIGHEST)
        inverse_root = jnp.dot(factor, inverse_root, precision=lax.Precision.HIGHEST)
    root_inverse = inverse_root / jnp.sqrt(bound_scale)
    mean_shift = jnp.dot(
        root_inverse,
        jnp.dot(root_inverse, drive_vector, precision=lax.Precision.HIGHEST),
        precision=lax.Precision.HIGHEST,
    )
    weights = jnp.sqrt(members - 1.0) * root_inverse.T + mean_shift[None, :]
    mixing = weights + (1.0 - jnp.sum(weights, axis=1))[:, None] / members
    return mixing.astype(jnp.bfloat16)


def local(prior_ensemble, measurement_anomaly_matrix, measured_per_portion, locality_support_marks):
    tile_count = lax.axis_size("tile")
    mem_count = lax.axis_size("mem")
    tile_index = lax.axis_index("tile")
    mem_index = lax.axis_index("mem")
    members = measurement_anomaly_matrix.shape[0] - 1
    obs_dev = measurement_anomaly_matrix.shape[1]
    gathered = with_halo(measurement_anomaly_matrix, (("tile", 1),), obs_dev)
    products = jnp.zeros((members + 1, members + 1), jnp.float32)
    for offset in range(3):
        source_tile = (tile_index + offset - 1 + tile_count) % tile_count
        root_weight = shard_weights(
            locality_support_marks,
            measured_per_portion,
            source_tile,
            mem_index,
            offset,
            obs_dev,
            mem_count,
        )
        segment = gathered[:, offset * obs_dev : (offset + 1) * obs_dev]
        products = products + gram_part(segment, root_weight)
    products = lax.psum(products, "mem")
    mixing = mixing_matrix(products, members)
    permuted_model_vector = lax.all_to_all(
        prior_ensemble, "mem", split_axis=1, concat_axis=0, tiled=True
    )
    return jnp.dot(mixing, permuted_model_vector, preferred_element_type=jnp.float32).astype(
        jnp.bfloat16
    )


def solution(mesh):
    placed = (P("mem", "tile"), P(None, ("tile", "mem")), P(), P())
    return jax.shard_map(
        local, mesh=mesh, in_specs=placed, out_specs=P(None, ("tile", "mem")), check_vma=False
    )
```

profile of v0, /device:TPU:1, one launch (start us, length us, event | category | flops | bytes accessed | tf_op | source)
XLA Modules:
  0.0 183.3 jit_solution(6382138974821264096)
XLA Ops:
  6.5 0.0 all-reduce.2.cloned.1.call-start
  6.5 6.9 %collective-permute-start.1 = (bf16[257,4096]{1,0:T(8,128)(2,1)}, bf16[257,4096]{1,0:T(8,128)(2,1)}, u32[]{:S(2)}, u32[]{:S(2)}) collective-permute-start(bf16[257,4096]{1,0:T(8,128)(2,1)} %param.5), channel_id=1, source_target_pairs={{16,0},{32,16},{48,32},{64,48},{80,64},{96,80},{112,96},{128,112},... | collective-permute-start | bytes 6316040 | tf_op jit(solution)/shard_map/ppermute | solution.py:21
  13.4 0.0 collective-permute-start
  13.4 1.5 fusion.39
  15.0 1.4 fusion.40
  16.5 0.1 compare_bitcast_fusion.1
  16.6 0.1 compare_bitcast_fusion.2
  16.6 0.1 compare_bitcast_fusion
  16.7 0.7 fusion.30
  17.4 1.3 fusion.26
  18.7 3.6 %fusion.1 = f32[257,257]{1,0:T(8,128)S(1)} fusion(bf16[257,4096]{1,0:T(8,128)(2,1)} %param.5, f32[4096]{0:T(1024)S(1)} %get-tuple-element.12), kind=kOutput, calls=%fused_computation.5 | convolution fusion | flops 544231424 | bytes 2385924 | tf_op jit(solution)/shard_map/dot_general | solution.py:47
  22.3 12.2 %collective-permute-done.1 = bf16[257,4096]{1,0:T(8,128)(2,1)} collective-permute-done((bf16[257,4096]{1,0:T(8,128)(2,1)}, bf16[257,4096]{1,0:T(8,128)(2,1)}, u32[]{:S(2)}, u32[]{:S(2)}) %collective-permute-start.1) | collective-permute-done | bytes 2105376 | tf_op jit(solution)/shard_map/ppermute | solution.py:21
  34.5 3.6 %fusion.2 = f32[257,257]{1,0:T(8,128)S(1)} fusion(bf16[257,4096]{1,0:T(8,128)(2,1)} %collective-permute-done.1, f32[4096]{0:T(1024)S(1)} %fusion.30), kind=kOutput, calls=%fused_computation.6 | convolution fusion | flops 544231424 | bytes 2385924 | tf_op jit(solution)/shard_map/dot_general | solution.py:47
  38.1 0.0 collective-permute-done
  38.1 0.0 copy-start
  38.1 2.1 %fusion.7 = f32[257,257]{1,0:T(8,128)} fusion(f32[257,257]{1,0:T(8,128)S(1)} %fusion.2, f32[257,257]{1,0:T(8,128)S(1)} %fusion.1, bf16[257,4096]{1,0:T(8,128)(2,1)S(1)} %collective-permute-done, f32[4096]{0:T(1024)S(1)} %get-tuple-element.11), kind=kOutput, calls=%fused_computation.11 | convolution fusion | flops 544363520 | bytes 2914316 | tf_op jit(solution)/shard_map/dot_general | solution.py:47
  40.2 0.0 all-reduce.2.cloned.1.call-update
  40.2 0.0 copy-done
  40.2 1.0 copy.9
  41.2 6.8 %all-to-all-start = ((bf16[16,16,2048]{2,0,1:T(8,128)(2,1)}), bf16[16,16,2048]{2,0,1:T(8,128)(2,1)S(1)}, u32[]{:S(2)}, u32[]{:S(2)}) async-start(bf16[16,16,2048]{2,0,1:T(8,128)(2,1)} %bitcast.73), calls=%async_computation | async-start | bytes 2097152 | tf_op jit(solution)/shard_map/all_to_all | solution.py:101
  48.0 112.6 %all-reduce.2.cloned.1.call-done = f32[257,257]{1,0:T(8,128)} async-done(((f32[257,257]{1,0:T(8,128)}), f32[257,257]{1,0:T(8,128)}) %all-reduce.2.cloned.1.call-update) | async-done | bytes 264212 | tf_op jit(solution)/shard_map/psum | solution.py:99
  160.6 0.0 copy-start.1
  160.6 1.1 abs_reduce_fusion
  161.7 0.6 reduce_max.9
  162.4 1.9 %fusion.15 = f32[256,256]{1,0:T(8,128)S(1)} fusion(f32[257,257]{1,0:T(8,128)} %all-reduce.2.cloned.1.call-done, f32[]{:T(128)} %reduce_max.9), kind=kOutput, calls=%fused_computation.28 | convolution fusion | flops 201916416 | bytes 524800 | tf_op jit(solution)/shard_map/dot_general | solution.py:61
  164.3 0.3 fusion.16
  164.6 0.0 copy-done.1
  164.6 1.0 fusion.22
  165.6 0.4 fusion.14
  166.0 0.4 fusion.42
  166.4 0.4 fusion.41
  166.7 0.4 fusion.13
  167.1 0.4 fusion.44
  167.5 0.4 fusion.43
  167.9 0.4 fusion.12
  168.3 0.4 fusion.46
  168.7 0.4 fusion.45
  169.1 0.4 fusion.11
  169.5 0.4 fusion.48
  169.8 0.4 fusion.47
  170.2 0.4 fusion.10
  170.6 0.4 fusion.50
  171.0 0.4 fusion.49
  171.4 0.4 fusion.9
  171.8 0.4 fusion.52
  172.2 0.4 fusion.51
  173.2 0.4 fusion.8
  173.6 0.4 convolution_divide_fusion
  174.0 0.1 slice_reduce_fusion
  174.1 0.3 convolution_bitcast_fusion
  174.4 0.3 fusion.53
  174.7 0.2 fusion.17
  174.9 0.0 all-to-all-done
  174.9 1.5 convolution_convert_fusion
  (1 shorter events, 0.0 us)
Async XLA Ops:
  6.5 154.1 %all-reduce.2.cloned.1.call-start = ((), (), s32[]{:S(2)}) async-start(), calls=%async_computation.1 | async-start | bytes 811008 | tf_op jit(solution)/shard_map/psum | solution.py:99
  6.5 28.0 %collective-permute-start.1 = (bf16[257,4096]{1,0:T(8,128)(2,1)}, bf16[257,4096]{1,0:T(8,128)(2,1)}, u32[]{:S(2)}, u32[]{:S(2)}) collective-permute-start(bf16[257,4096]{1,0:T(8,128)(2,1)} %param.5), channel_id=1, source_target_pairs={{16,0},{32,16},{48,32},{64,48},{80,64},{96,80},{112,96},{128,112},... | collective-permute-start | bytes 6316040 | tf_op jit(solution)/shard_map/ppermute | solution.py:21
  13.4 24.6 %collective-permute-start = (bf16[257,4096]{1,0:T(8,128)(2,1)}, bf16[257,4096]{1,0:T(8,128)(2,1)S(1)}, u32[]{:S(2)}, u32[]{:S(2)}) collective-permute-start(bf16[257,4096]{1,0:T(8,128)(2,1)} %param.5), channel_id=1, source_target_pairs={{0,16},{16,32},{32,48},{48,64},{64,80},{80,96},{96,112},{112,128},... | collective-permute-start | bytes 6316040 | tf_op jit(solution)/shard_map/ppermute | solution.py:19
  38.1 2.1 %copy-start = (bf16[16,32768]{1,0:T(8,128)(2,1)S(1)}, bf16[16,32768]{1,0:T(8,128)(2,1)}, u32[]{:S(2)}) copy-start(bf16[16,32768]{1,0:T(8,128)(2,1)} %param.4) | copy-start | bytes 3145732
  41.2 133.7 %all-to-all-start = ((bf16[16,16,2048]{2,0,1:T(8,128)(2,1)}), bf16[16,16,2048]{2,0,1:T(8,128)(2,1)S(1)}, u32[]{:S(2)}, u32[]{:S(2)}) async-start(bf16[16,16,2048]{2,0,1:T(8,128)(2,1)} %bitcast.73), calls=%async_computation | async-start | bytes 2097152 | tf_op jit(solution)/shard_map/all_to_all | solution.py:101
  160.6 4.0 %copy-start.1 = (f32[257,257]{1,0:T(8,128)S(1)}, f32[257,257]{1,0:T(8,128)}, u32[]{:S(2)}) copy-start(f32[257,257]{1,0:T(8,128)} %all-reduce.2.cloned.1.call-done) | copy-start | bytes 792592
Sparse Core Ops, SparseCore 0:
  40.3 120.2 all-reduce.1
where the time goes:
time: 184 us; the launch traced here: 183 us
  waiting for transfers between devices  125 us (68%)
  matrix products  22.1 us (12%)
  between operations  14.4 us (8%)
  starting transfers between devices  13.6 us (7%)
  other arithmetic  4.2 us (2%)
  local copies, waits for them, and re-layouts  4.08 us (2%)
    psum x1, waiting for transfers between devices, local(): products = lax.psum(products, 'mem')  113 us
    ppermute x1, waiting for transfers between devices, with_halo(): lax.ppermute(head, axis, [((i + 1) % count, i) for i in range(count)])  12.2 us
    dot_general x3, matrix products, gram_part(): lax.dot_general(scaled, scaled, (((1,), (1,)), ((), ())), preferred_eleme...  9.2 us
    ppermute x1, starting transfers between devices, with_halo(): lax.ppermute(head, axis, [((i + 1) % count, i) for i in range(count)])  6.88 us
    all_to_all x1, starting transfers between devices, local(): lax.all_to_all(prior_ensemble, 'mem', split_axis=1, concat_axis=0, tiled=...  6.76 us
    dot_general x8, matrix products, mixing_matrix(): jnp.dot(inverse_root, iterate, precision=lax.Precision.HIGHEST)  4.57 us
  transfers between devices with their start and end apart: 4, of which 2 were waited for; matrix products, arithmetic and copies ran while one was open for 15% of the time, Pallas kernels for 0%

commit v1 on v0

v1 whole, which is shorter than its diff:
```python
import functools

import jax
import jax.numpy as jnp
from jax import lax
from jax.experimental import pallas as pl
from jax.experimental.pallas import tpu as pltpu
from jax.sharding import PartitionSpec as P

MESH = pl.DeviceIdType.MESH
NS_STEPS = 8
LANES = 128
CHUNKS = 4


def split(x):
    high = x.astype(jnp.bfloat16)
    return high, (x - high.astype(jnp.float32)).astype(jnp.bfloat16)


def product(left, right):
    (lh, ll), (rh, rl) = left, right
    return jnp.dot(
        jnp.concatenate([lh, ll, lh], axis=1),
        jnp.concatenate([rh, rh, rl], axis=0),
        preferred_element_type=jnp.float32,
    )


def kernel(
    n_tile,
    n_mem,
    counts,
    prior,
    obs,
    marks,
    mixing_out,
    gathered,
    obs_v,
    marks_v,
    marks_t,
    weight_v,
    scaled_v,
    cross_out,
    inner_out,
    cross_in,
    inner_in,
    total,
    parts_in,
    system_v,
    local_sem,
    obs_sem,
    pair_send,
    pair_recv,
    rs_send,
    rs_recv,
    ag_send,
    ag_recv,
    a2a_send,
    a2a_recv,
):
    tile = lax.axis_index("tile")
    mem = lax.axis_index("mem")
    members = mixing_out.shape[0]
    half = members // 2
    obs_dev = obs.shape[1]
    blocks = obs_dev // LANES
    part = half // n_mem
    own_rows = prior.shape[0]
    own_cols = gathered.shape[1]

    cross_offset = 1 - 2 * lax.rem(tile, 2)
    cross_tile = lax.rem(tile - cross_offset + n_tile, n_tile)
    inner_tile = lax.rem(tile + cross_offset + n_tile, n_tile)
    peers = [lax.rem(mem + k, n_mem) for k in range(1, n_mem)]

    first_block = (tile * n_mem + mem) * blocks
    aligned = pl.multiple_of((first_block // LANES) * LANES, LANES)
    inside = pl.multiple_of(lax.rem(first_block, LANES), blocks)
    marks_copy = pltpu.make_async_copy(
        marks.at[:, pl.ds(aligned, LANES)], marks_v, local_sem.at[0]
    )
    marks_copy.start()
    width = obs_dev // CHUNKS
    obs_copies = [
        pltpu.make_async_copy(
            obs.at[:, pl.ds(c * width, width)], obs_v.at[:, pl.ds(c * width, width)], obs_sem.at[c]
        )
        for c in range(CHUNKS)
    ]
    for copy in obs_copies:
        copy.start()

    barrier = pltpu.get_barrier_semaphore()
    for other in (cross_tile, inner_tile):
        pl.semaphore_signal(barrier, inc=1, device_id=(other, mem), device_id_type=MESH)
    for peer in peers:
        pl.semaphore_signal(barrier, inc=1, device_id=(tile, peer), device_id_type=MESH)

    marks_copy.wait()
    alive_count = counts[tile * n_mem + mem]
    slot = (
        lax.broadcasted_iota(jnp.int32, (blocks, LANES), 0) * LANES
        + lax.broadcasted_iota(jnp.int32, (blocks, LANES), 1)
    )
    alive = slot < alive_count
    position = ((mem * obs_dev + slot).astype(jnp.float32) + 0.5) / (obs_dev * n_mem)
    offsets = (cross_offset, -cross_offset, 0)
    for index, offset in enumerate(offsets):
        row = marks_v[pl.ds(offset + 1, 1), :].astype(jnp.float32)
        marks_t[index] = jnp.broadcast_to(row, (LANES, LANES)).T
        pattern = marks_t[index, pl.ds(inside, blocks), :]
        distance = jnp.asarray(offset, jnp.float32) + position - 0.5
        smooth = jnp.exp(-0.5 * distance * distance)
        weight_v[index] = jnp.where(alive & (pattern > 0), smooth, jnp.zeros_like(smooth))

    def gram(index):
        for c in range(CHUNKS):
            if index == 0:
                obs_copies[c].wait()
            for b in range(c * blocks // CHUNKS, (c + 1) * blocks // CHUNKS):
                columns = pl.ds(b * LANES, LANES)
                weight = weight_v[index, pl.ds(b, 1), :]
                scaled_v[pl.ds(0, members), columns] = (
                    obs_v[pl.ds(0, members), columns].astype(jnp.float32) * weight
                ).astype(jnp.bfloat16)
                innovation = obs_v[pl.ds(members, 1), columns].astype(jnp.float32) * weight
                scaled_v[pl.ds(members, 16), columns] = jnp.broadcast_to(
                    innovation, (16, LANES)
                ).astype(jnp.bfloat16)
        return lax.dot_general(
            scaled_v[...],
            scaled_v[pl.ds(0, members), :],
            (((1,), (1,)), ((), ())),
            preferred_element_type=jnp.float32,
        )

    def packed(products):
        upper = products[:half, :half]
        drive = products[members : members + 1, :]
        left, right = drive[:, :half], drive[:, half:]
        rows = jnp.concatenate(
            [
                left,
                pltpu.roll(left, half // 2, 1),
                right,
                pltpu.roll(right, half // 2, 1),
                jnp.zeros((4, half), jnp.float32),
            ],
            axis=0,
        )
        lane = lax.broadcasted_iota(jnp.int32, (8, half), 1)
        last = jnp.where(lane < half // 2, rows, upper[half - 8 :])
        upper = jnp.concatenate([upper[: half - 8], last], axis=0)
        return [
            block.reshape(n_mem, part, half)
            for block in (upper, products[:half, half:], products[half:members, half:])
        ]

    def put(ref, blocks_of):
        for i, block in enumerate(blocks_of):
            ref[:, pl.ds(i * part, part), :] = block

    put(cross_out, packed(gram(0)))
    pl.semaphore_wait(barrier, n_mem + 1)
    cross = pltpu.make_async_remote_copy(
        cross_out, cross_in, pair_send.at[0], pair_recv.at[0], (cross_tile, mem), MESH
    )
    cross.start()
    put(inner_out, packed(gram(1)))
    inner = pltpu.make_async_remote_copy(
        inner_out, inner_in, pair_send.at[1], pair_recv.at[1], (inner_tile, mem), MESH
    )
    inner.start()
    put(total, packed(gram(2)))
    inner.wait_recv()
    cross.wait_recv()
    total[...] += inner_in[...] + cross_in[...]

    scatter = [
        pltpu.make_async_remote_copy(
            total.at[peer],
            parts_in.at[k],
            rs_send.at[k],
            rs_recv.at[k],
            (tile, peer),
            MESH,
        )
        for k, peer in enumerate(peers)
    ]
    for copy in scatter:
        copy.start()
    mine = total[mem]
    for k, copy in enumerate(scatter):
        copy.wait_recv()
        mine = mine + parts_in[k]
    system_v[mem] = mine
    share = [
        pltpu.make_async_remote_copy(
            system_v.at[mem],
            system_v.at[mem],
            ag_send.at[k],
            ag_recv.at[k],
            (tile, peer),
            MESH,
        )
        for k, peer in enumerate(peers)
    ]
    for copy in share:
        copy.start()

    home = gathered.at[pl.ds(pl.multiple_of(mem * own_rows, own_rows), own_rows), :]

    def cells(owner):
        return prior.at[:, pl.ds(pl.multiple_of(owner * own_cols, own_cols), own_cols)]

    spread = [
        pltpu.make_async_remote_copy(
            cells(peer), home, a2a_send.at[k], a2a_recv.at[k], (tile, peer), MESH
        )
        for k, peer in enumerate(peers)
    ]
    keep = pltpu.make_async_copy(cells(mem), home, local_sem.at[1])
    for copy in spread:
        copy.start()
    keep.start()

    for copy in share:
        copy.wait_recv()
    upper, side, lower = (
        system_v[:, pl.ds(i * part, part), :].reshape(half, half) for i in range(3)
    )
    corner = upper[half - 8 :]
    lane = lax.broadcasted_iota(jnp.int32, (1, half), 1)
    drive = jnp.concatenate(
        [
            jnp.where(lane < half // 2, corner[i : i + 1], pltpu.roll(corner[i + 1 : i + 2], half // 2, 1))
            for i in (0, 2)
        ],
        axis=1,
    )
    above = lax.broadcasted_iota(jnp.int32, (half, half), 1) >= lax.broadcasted_iota(
        jnp.int32, (half, half), 0
    )
    upper = jnp.where(above, upper, upper.T)
    gram_block = jnp.concatenate(
        [
            jnp.concatenate([upper, side], axis=1),
            jnp.concatenate([side.T, lower], axis=1),
        ],
        axis=0,
    )
    diagonal = lax.broadcasted_iota(jnp.int32, (members, members), 0) == lax.broadcasted_iota(
        jnp.int32, (members, members), 1
    )
    identity = diagonal.astype(jnp.float32)
    system = (members - 1.0) * identity + gram_block
    bound = jnp.max(jnp.sum(jnp.abs(system), axis=1, keepdims=True), axis=0, keepdims=True)
    both = system / bound
    inverse_root = None
    for sweep in range(NS_STEPS):
        factor = 1.5 * identity - 0.5 * both
        halves = split(factor)
        if sweep < NS_STEPS - 1:
            once = product(split(both), halves)
        inverse_root = factor if sweep == 0 else product(split(inverse_root), halves)
        if sweep < NS_STEPS - 1:
            both = product(split(once), halves)
    inner_shift = jnp.sum(inverse_root * drive, axis=1, keepdims=True)
    mean_shift = jnp.sum(inverse_root * inner_shift, axis=0, keepdims=True) / bound
    weights = inverse_root * (jnp.sqrt(members - 1.0) * lax.rsqrt(bound)) + mean_shift
    mixing = weights + (1.0 - jnp.sum(weights, axis=1, keepdims=True)) / members
    mixing_out[...] = mixing.astype(jnp.bfloat16)

    keep.wait()
    for copy in spread:
        copy.wait_recv()
    for copy in [cross, inner, *scatter, *share, *spread]:
        copy.wait_send()


def solution(mesh):
    n_tile, n_mem = mesh.shape["tile"], mesh.shape["mem"]

    def local(prior, obs, counts, marks):
        members = obs.shape[0] - 1
        half = members // 2
        obs_dev = obs.shape[1]
        blocks = obs_dev // LANES
        packed_shape = (n_mem, 3 * half // n_mem, half)
        dma = pltpu.SemaphoreType.DMA
        mixing, gathered = pl.pallas_call(
            functools.partial(kernel, n_tile, n_mem),
            out_shape=(
                jax.ShapeDtypeStruct((members, members), jnp.bfloat16),
                jax.ShapeDtypeStruct((members, prior.shape[1] // n_mem), jnp.bfloat16),
            ),
            in_specs=[
                pl.BlockSpec(memory_space=pltpu.SMEM),
                pl.BlockSpec(memory_space=pl.ANY),
                pl.BlockSpec(memory_space=pl.ANY),
                pl.BlockSpec(memory_space=pl.ANY),
            ],
            out_specs=(
                pl.BlockSpec(memory_space=pltpu.VMEM),
                pl.BlockSpec(memory_space=pl.ANY),
            ),
            scratch_shapes=[
                pltpu.VMEM(obs.shape, jnp.bfloat16),
                pltpu.VMEM((3, LANES), jnp.int32),
                pltpu.VMEM((3, LANES, LANES), jnp.float32),
                pltpu.VMEM((3, blocks, LANES), jnp.float32),
                pltpu.VMEM((members + 16, obs_dev), jnp.bfloat16),
                pltpu.VMEM(packed_shape, jnp.float32),
                pltpu.VMEM(packed_shape, jnp.float32),
                pltpu.VMEM(packed_shape, jnp.float32),
                pltpu.VMEM(packed_shape, jnp.float32),
                pltpu.VMEM(packed_shape, jnp.float32),
                pltpu.VMEM((n_mem - 1, *packed_shape[1:]), jnp.float32),
                pltpu.VMEM(packed_shape, jnp.float32),
                dma((2,)),
                dma((CHUNKS,)),
                dma((2,)),
                dma((2,)),
                dma((n_mem - 1,)),
                dma((n_mem - 1,)),
                dma((n_mem - 1,)),
                dma((n_mem - 1,)),
                dma((n_mem - 1,)),
                dma((n_mem - 1,)),
            ],
            compiler_params=pltpu.CompilerParams(
                collective_id=0, has_side_effects=True, vmem_limit_bytes=32 * 1024 * 1024
            ),
        )(counts, prior, obs, marks)
        return jnp.dot(mixing, gathered, preferred_element_type=jnp.float32).astype(jnp.bfloat16)

    placed = (P("mem", "tile"), P(None, ("tile", "mem")), P(), P())
    return jax.shard_map(
        local, mesh=mesh, in_specs=placed, out_specs=P(None, ("tile", "mem")), check_vma=False
    )
```

time: 184 us -> 44.1 us (0.24)
  waiting for transfers between devices: 125 us -> 0 us
  Pallas kernels: 0 us -> 38 us
  matrix products: 22.1 us -> 1.41 us
  between operations: 14.4 us -> 0.01 us
  starting transfers between devices: 13.6 us -> 0 us
  other arithmetic: 4.2 us -> 0 us
    psum x1 -> x0, waiting for transfers between devices: 113 us -> none  [local(): products = lax.psum(products, 'mem')]
    pallas_call x0 -> x1, Pallas kernels: none -> 38 us  [local(): pl.pallas_call(functools.partial(kernel, n_tile, n_mem), out_shape=(jax.S...]
    dot_general x29 -> x1, matrix products: 22.1 us -> 1.41 us  [local(): jnp.dot(mixing, gathered, preferred_element_type=jnp.float32)]
    ppermute x2 -> x0, waiting for transfers between devices: 12.2 us -> none  [the longest x1 12.2 us: with_halo(): lax.ppermute(head, axis, [((i + 1) % count, i) for i in range(count)])]
    ppermute x2 -> x0, starting transfers between devices: 6.88 us -> none  [the longest x1 6.88 us: with_halo(): lax.ppermute(head, axis, [((i + 1) % count, i) for i in range(count)])]
    all_to_all x1 -> x0, starting transfers between devices: 6.76 us -> none  [local(): lax.all_to_all(prior_ensemble, 'mem', split_axis=1, concat_axis=0, tiled=...]
    unnamed x4 -> x8, local copies, waits for them, and re-layouts: 0.01 us -> 4.46 us
    select_n x2 -> x0, other arithmetic: 2.04 us -> none  [shard_weights(): jnp.where(alive_mask & (pattern_rows > 0), smooth, jnp.zeros_like(smooth))]
  transfers between devices with their start and end apart: 4 -> 0, of which waited for: 2 -> 0; matrix products, arithmetic and copies ran while one was open for 15% -> 0% of each run, Pallas kernels for 0% -> 0%
where the time goes in v1:
time: 44.1 us; the launch traced here: 43.9 us
  Pallas kernels  38 us (86%)
  local copies, waits for them, and re-layouts  4.46 us (10%)
  matrix products  1.41 us (3%)
    pallas_call x1, Pallas kernels, local(): pl.pallas_call(functools.partial(kernel, n_tile, n_mem), out_shape=(jax.S...  38 us
    unnamed x8, local copies, waits for them, and re-layouts  4.46 us
    dot_general x1, matrix products, local(): jnp.dot(mixing, gathered, preferred_element_type=jnp.float32)  1.41 us

profile of v1, /device:TPU:1, one launch (start us, length us, event | category | flops | bytes accessed | tf_op | source)
XLA Modules:
  0.0 43.9 jit_solution(14607273112007644635)
XLA Ops:
  0.0 0.0 copy-start
  0.0 1.6 %copy-done = bf16[257,4096]{1,0:T(8,128)(2,1)S(1)} copy-done((bf16[257,4096]{1,0:T(8,128)(2,1)S(1)}, bf16[257,4096]{1,0:T(8,128)(2,1)}, u32[]{:S(2)}) %copy-start) | copy-done | bytes 2105368
  1.6 0.0 copy-start.1
  1.6 1.2 %copy-done.1 = bf16[16,32768]{1,0:T(8,128)(2,1)S(1)} copy-done((bf16[16,32768]{1,0:T(8,128)(2,1)S(1)}, bf16[16,32768]{1,0:T(8,128)(2,1)}, u32[]{:S(2)}) %copy-start.1) | copy-done | bytes 1048600
  2.8 0.0 copy-start.2
  2.8 0.9 %copy-done.2 = s32[3,16384]{1,0:T(4,128)S(1)} copy-done((s32[3,16384]{1,0:T(4,128)S(1)}, s32[3,16384]{1,0:T(4,128)}, u32[]{:S(2)}) %copy-start.2) | copy-done | bytes 196632
  3.8 0.0 copy-start.3
  3.8 0.7 %copy-done.3 = s32[512]{0:T(512)S(1)} copy-done((s32[512]{0:T(512)S(1)}, s32[512]{0:T(512)}, u32[]{:S(2)}) %copy-start.3) | copy-done | bytes 2072
  4.5 38.0 %shard_map.46 = (bf16[256,256]{1,0:T(8,128)(2,1)S(1)}, bf16[256,2048]{1,0:T(8,128)(2,1)S(1)}) custom-call(s32[512]{0:T(512)S(1)} %copy-done.3, bf16[16,32768]{1,0:T(8,128)(2,1)S(1)} %copy-done.1, bf16[257,4096]{1,0:T(8,128)(2,1)S(1)} %copy-done, s32[3,16384]{1,0:T(4,128)S(1)} %copy-done.2), custom_call_target="tpu_custom_call" | custom-call | tf_op jit(solution)/shard_map/pallas_call | solution.py:292
  42.4 1.4 %convolution_convert_fusion = bf16[256,2048]{1,0:T(8,128)(2,1)} fusion(bf16[256,256]{1,0:T(8,128)(2,1)S(1)} %get-tuple-element.7, bf16[256,2048]{1,0:T(8,128)(2,1)S(1)} %get-tuple-element.8), kind=kOutput, calls=%fused_computation | convolution fusion | flops 268959744 | bytes 2228224 | tf_op jit(solution)/shard_map/dot_general | solution.py:336
Async XLA Ops:
  0.0 1.6 %copy-start = (bf16[257,4096]{1,0:T(8,128)(2,1)S(1)}, bf16[257,4096]{1,0:T(8,128)(2,1)}, u32[]{:S(2)}) copy-start(bf16[257,4096]{1,0:T(8,128)(2,1)} %obs.1) | copy-start | bytes 6316036
  1.6 1.2 %copy-start.1 = (bf16[16,32768]{1,0:T(8,128)(2,1)S(1)}, bf16[16,32768]{1,0:T(8,128)(2,1)}, u32[]{:S(2)}) copy-start(bf16[16,32768]{1,0:T(8,128)(2,1)} %prior.1) | copy-start | bytes 3145732
  2.8 0.9 %copy-start.2 = (s32[3,16384]{1,0:T(4,128)S(1)}, s32[3,16384]{1,0:T(4,128)}, u32[]{:S(2)}) copy-start(s32[3,16384]{1,0:T(4,128)} %marks.1) | copy-start | bytes 589828
  3.8 0.7 %copy-start.3 = (s32[512]{0:T(512)S(1)}, s32[512]{0:T(512)}, u32[]{:S(2)}) copy-start(s32[512]{0:T(512)} %counts.1) | copy-start | bytes 6148
